TPU v7x, 32 devices: a whole 2x2x4 slice. The times are simulated.
32 devices in a mesh: groups: 2 (over x), seq: 16 (over z, y, core).
Axes of the slice: x: 2, y: 2, z: 4, core: 2. Of those that a mesh axis runs over, the one named last changes fastest.
Arguments:
- queries: bfloat16 [4, 1024, 1024], P('groups', 'seq'), parts along dimension 0, may hold values from -6 to 6
- keys: bfloat16 [4, 1024, 1024], P('groups', 'seq'), parts along dimension 0, may hold values from -6 to 6
- values: bfloat16 [4, 1024, 1024], P('groups', 'seq'), parts along dimension 0, may hold values from -6 to 6
- resid: bfloat16 [4, 1024, 2048], P('groups', 'seq'), parts along dimension 0, may hold values from -3 to 3
- w_out: bfloat16 [1024, 2048], P('seq'), may hold values from -0.1875 to 0.1875
- w_head: bfloat16 [2048, 256], replicated, may hold values from -0.125 to 0.125
- target: float32 [2048, 256], P(('groups', 'seq')), parts along dimension 0, may hold values from -18 to 18
- block_ids: int32 [2048], P(('groups', 'seq')), parts along dimension 0, may hold values from 0 to 63, never falling along the last dimension, each value on 1 to 32 neighbouring positions
Outputs:
- loss: float32 [2], P('groups'), parts along dimension 0
- d_queries: bfloat16 [4, 1024, 1024], P('groups', 'seq'), parts along dimension 0
- d_keys: bfloat16 [4, 1024, 1024], P('groups', 'seq'), parts along dimension 0
- d_values: bfloat16 [4, 1024, 1024], P('groups', 'seq'), parts along dimension 0
- d_w_out: float32 [2048, 2048], P(('groups', 'seq')), parts along dimension 0
- d_w_head: float32 [4096, 256], P('groups'), parts along dimension 0
There are 2 independent parts, one for each index of `groups`. A program takes and returns all parts, laid end to end along the dimension named above; an argument that names none is the same for every part. Nothing has to cross between parts.
Inputs may be any that keep to these rules, and one draw needn't show every extreme that they name: `block_ids`: never falling along the positions; every block number from 0 to 63 occurs, each block covers 1 to 32 positions and one covers exactly 32. Block 63 borders block 0.
All inputs are finite; a program needn't handle non-finite values.
Results may differ from a plain program's by a relative error of at most 0.0087.
Values may be sent and summed in bfloat16 or wider, within the bound.
A program may use at most 64 MiB of HBM per device.

v0:
```python
import jax
import jax.numpy as jnp
from jax import lax
from jax.sharding import PartitionSpec as P

DH = 128


def passed_along(x, axis, by):
    peers = lax.axis_size(axis)
    return lax.ppermute(x, axis, [(i, (i + by) % peers) for i in range(peers)])


def link_mask(query_ids, key_ids, number):
    gap = (query_ids[:, None] - key_ids[None, :]) % number
    return (gap == 0) | (gap == 1) | (gap == number - 1)


def ensemble_score(predicted, target):
    members = predicted.shape[0]
    offset_t = predicted - target[None]
    soft = jnp.sqrt(1.0 + offset_t * offset_t)
    pairwise = predicted[:, None] - predicted[None, :]
    soft_pair = jnp.sqrt(1.0 + pairwise * pairwise)
    score = jnp.sum(soft - 1.0) / members - jnp.sum(soft_pair - 1.0) / (2 * members * (members - 1))
    gradient = offset_t / soft / members - jnp.sum(pairwise / soft_pair, axis=1) / (
        members * (members - 1)
    )
    return (score, gradient)


def masked_scores(query_part, key_part, allowed, scaling):
    scores = (
        jnp.einsum("qhd,khd->hqk", query_part, key_part, preferred_element_type=jnp.float32)
        * scaling
    )
    return jnp.where(allowed[None], scores, -1e30)


def per_device(queries, keys, values, resid, w_out, w_head, target, block_ids):
    members, tok_rows, hd_width = queries.shape
    heads = hd_width // DH
    cycle_size = lax.axis_size("seq")
    number = 4 * cycle_size
    scaling = DH ** (-0.5)

    def split_heads(array):
        return array.reshape(array.shape[0], heads, DH)

    ids_half = block_ids.astype(jnp.bfloat16)
    from_left = passed_along((keys, values, ids_half), "seq", 1)
    from_right = passed_along((keys, values, ids_half), "seq", -1)
    left_ids = from_left[2].astype(jnp.int32)
    right_ids = from_right[2].astype(jnp.int32)
    window_keys = jnp.concatenate([from_left[0], keys, from_right[0]], axis=1)
    window_values = jnp.concatenate([from_left[1], values, from_right[1]], axis=1)
    allowed = link_mask(block_ids, jnp.concatenate([left_ids, block_ids, right_ids]), number)
    prob_list, half_list, peak_list, total_list, attended_list = ([], [], [], [], [])
    for member in range(members):
        scores = masked_scores(
            split_heads(queries[member]), split_heads(window_keys[member]), allowed, scaling
        )
        peak = jnp.max(scores, axis=-1, keepdims=True)
        exponent = jnp.exp(scores - peak)
        totals = jnp.sum(exponent, axis=-1, keepdims=True)
        probs = exponent / totals
        probs_half = probs.astype(jnp.bfloat16)
        attended = jnp.einsum(
            "hqk,khd->qhd",
            probs_half,
            split_heads(window_values[member]),
            preferred_element_type=jnp.float32,
        )
        attended_list.append(attended.astype(jnp.bfloat16).reshape(tok_rows, hd_width))
        prob_list.append(probs)
        half_list.append(probs_half)
        peak_list.append(peak)
        total_list.append(totals)
    attn_flat = jnp.stack(attended_list).reshape(members * tok_rows, hd_width)
    whole_out = lax.all_gather(w_out, "seq", axis=0, tiled=True)
    projected = jnp.dot(attn_flat, whole_out, preferred_element_type=jnp.float32)
    mixed = (resid.reshape(members * tok_rows, -1).astype(jnp.float32) + projected).astype(
        jnp.bfloat16
    )
    predicted = jnp.dot(mixed, w_head, preferred_element_type=jnp.float32).reshape(
        members, tok_rows, -1
    )
    crps_sum, gradient = ensemble_score(predicted, target)
    d_pred = gradient.astype(jnp.bfloat16).reshape(members * tok_rows, -1)
    head_local = jnp.einsum("rd,rv->dv", mixed, d_pred, preferred_element_type=jnp.float32)
    score_total, d_w_head = lax.psum((crps_sum, head_local), "seq")
    loss = (score_total / (cycle_size * tok_rows * predicted.shape[2])).reshape(1)
    d_mixed = jnp.einsum("rv,dv->rd", d_pred, w_head, preferred_element_type=jnp.float32).astype(
        jnp.bfloat16
    )
    attended_pred = lax.psum_scatter(
        jnp.einsum("rh,rv->hv", attn_flat, d_pred, preferred_element_type=jnp.float32),
        "seq",
        scatter_dimension=0,
        tiled=True,
    )
    d_w_out = jnp.dot(attended_pred, w_head.astype(jnp.float32).T, precision=lax.Precision.HIGHEST)
    d_attn = jnp.einsum("rd,hd->rh", d_mixed, whole_out, preferred_element_type=jnp.float32)
    d_attn = d_attn.astype(jnp.bfloat16).reshape(members, tok_rows, hd_width)
    dq_list, dk_list, dv_list, delta_list = ([], [], [], [])
    for member in range(members):
        grad_heads = split_heads(d_attn[member])
        query_heads = split_heads(queries[member])
        d_probs = jnp.einsum(
            "qhd,khd->hqk",
            grad_heads,
            split_heads(window_values[member]),
            preferred_element_type=jnp.float32,
        )
        delta = jnp.sum(prob_list[member] * d_probs, axis=-1, keepdims=True)
        d_scores = (prob_list[member] * (d_probs - delta) * scaling).astype(jnp.bfloat16)
        d_query = jnp.einsum(
            "hqk,khd->qhd",
            d_scores,
            split_heads(window_keys[member]),
            preferred_element_type=jnp.float32,
        )
        dq_list.append(d_query.astype(jnp.bfloat16).reshape(tok_rows, hd_width))
        delta_list.append(delta)
        prob_part = half_list[member]
        d_key = jnp.einsum(
            "hqk,qhd->khd", d_scores, query_heads, preferred_element_type=jnp.float32
        )
        d_value = jnp.einsum(
            "hqk,qhd->khd", prob_part, grad_heads, preferred_element_type=jnp.float32
        )
        dk_list.append(d_key.reshape(d_key.shape[0], hd_width))
        dv_list.append(d_value.reshape(d_value.shape[0], hd_width))
    d_queries = jnp.stack(dq_list)
    key_terms = jnp.stack(dk_list)
    value_terms = jnp.stack(dv_list)
    to_left = (key_terms[:, :tok_rows], value_terms[:, :tok_rows])
    to_right = (key_terms[:, 2 * tok_rows :], value_terms[:, 2 * tok_rows :])
    got_next = (
        passed_along(to_left[0].astype(jnp.bfloat16), "seq", -1).astype(jnp.float32),
        passed_along(to_left[1].astype(jnp.bfloat16), "seq", -1).astype(jnp.float32),
    )
    got_prior = passed_along((to_right[0], to_right[1]), "seq", 1)
    key_sum = key_terms[:, tok_rows : 2 * tok_rows] + got_next[0] + got_prior[0]
    value_sum = value_terms[:, tok_rows : 2 * tok_rows] + got_next[1] + got_prior[1]
    d_keys = key_sum.astype(jnp.bfloat16)
    d_values = value_sum.astype(jnp.bfloat16)
    return (loss, d_queries, d_keys, d_values, d_w_out, d_w_head)


def solution(mesh):
    return jax.shard_map(
        per_device,
        mesh=mesh,
        in_specs=(
            P("groups", "seq", None),
            P("groups", "seq", None),
            P("groups", "seq", None),
            P("groups", "seq", None),
            P("seq", None),
            P(),
            P(("groups", "seq"), None),
            P(("groups", "seq")),
        ),
        out_specs=(
            P("groups"),
            P("groups", "seq", None),
            P("groups", "seq", None),
            P("groups", "seq", None),
            P(("groups", "seq"), None),
            P("groups", None),
        ),
        check_vma=False,
    )
```

profile of v0, /device:TPU:0, one launch (start us, length us, event | category | flops | bytes accessed | tf_op | source)
XLA Modules:
  0.0 263.2 jit_solution(16274518420779684170)
XLA Ops:
  8.6 5.4 %collective-permute-start.3 = (bf16[64]{0:T(256)(128)(2,1)S(1)}, bf16[64]{0:T(256)(128)(2,1)S(1)}, u32[]{:S(2)}, u32[]{:S(2)}) collective-permute-start(bf16[64]{0:T(256)(128)(2,1)S(1)} %convert_element_type.83), channel_id=1, source_target_pairs={{0,15},{1,0},{2,1},{3,2},{4,3},{5,4},{6,5},{7,6},{8,7},{9,8},{10,9... | collective-permute-start | bytes 392 | tf_op jit(solution)/shard_map/ppermute | solution.py:11
  14.1 4.5 %collective-permute-start.5 = (bf16[2,64,1024]{2,1,0:T(8,128)(2,1)}, bf16[2,64,1024]{2,1,0:T(8,128)(2,1)S(1)}, u32[]{:S(2)}, u32[]{:S(2)}) collective-permute-start(bf16[2,64,1024]{2,1,0:T(8,128)(2,1)} %param.9), channel_id=1, source_target_pairs={{0,15},{1,0},{2,1},{3,2},{4,3},{5,4},{6,5},{7,6},{8,7},{9,8},{10,9... | collective-permute-start | bytes 786440 | tf_op jit(solution)/shard_map/ppermute | solution.py:11
  20.3 4.4 %collective-permute-start.1 = (bf16[2,64,1024]{2,1,0:T(8,128)(2,1)}, bf16[2,64,1024]{2,1,0:T(8,128)(2,1)S(1)}, u32[]{:S(2)}, u32[]{:S(2)}) collective-permute-start(bf16[2,64,1024]{2,1,0:T(8,128)(2,1)} %param.10), channel_id=1, source_target_pairs={{0,15},{1,0},{2,1},{3,2},{4,3},{5,4},{6,5},{7,6},{8,7},{9,8},{10,9... | collective-permute-start | bytes 786440 | tf_op jit(solution)/shard_map/ppermute | solution.py:11
  26.2 2.5 collective-permute-done
  37.4 28.5 %all-gather.2.cloned.1.call-done = bf16[1024,2048]{1,0:T(8,128)(2,1)} async-done(((bf16[64,2048]{1,0:T(8,128)(2,1)}), bf16[1024,2048]{1,0:T(8,128)(2,1)}) %all-gather.2.cloned.1.call-update) | async-done | bytes 4194320 | tf_op jit(solution)/shard_map/all_gather | solution.py:80
  65.8 3.0 %fusion.4 = bf16[128,2048]{1,0:T(8,128)(2,1)S(1)} fusion(bf16[128,1024]{1,0:T(8,128)(2,1)S(1)} %bitcast.99, bf16[1024,2048]{1,0:T(8,128)(2,1)} %all-gather.2.cloned.1.call-done, bf16[128,2048]{1,0:T(8,128)(2,1)} %bitcast.104), kind=kOutput, calls=%fused_computation.5 | convolution fusion | flops 537657344 | bytes 5505024 | tf_op jit(solution)/shard_map/dot_general | solution.py:81
  70.7 4.1 %fusion.22 = bf16[128,1024]{1,0:T(8,128)(2,1)S(1)} fusion(bf16[1024,2048]{1,0:T(8,128)(2,1)} %all-gather.2.cloned.1.call-done, bf16[128,256]{1,0:T(8,128)(2,1)S(1)} %get-tuple-element.16, bf16[2048,256]{1,0:T(8,128)(2,1)S(1)} %copy-done), kind=kOutput, calls=%fused_computation.31 | convolution fusion | flops 671481856 | bytes 5570560 | tf_op jit(solution)/shard_map/rd,hd->rh/dot_general | solution.py:103
  76.6 3.3 %convolution_bitcast_fusion.2 = f32[192,8,128]{2,0,1:T(8,128)} fusion(bf16[8,8,8,128]{3,2,1,0:T(8,128)(2,1)S(1)} %get-tuple-element.12, f32[8,64]{1,0:T(8,128)S(1)} %get-tuple-element.18, f32[8,64,192]{2,1,0:T(8,128)} %copy-done.6), kind=kOutput, calls=%fused_computation.11 | convolution fusion | flops 25461440 | bytes 1312768 | tf_op jit(solution)/shard_map/hqk,qhd->khd/dot_general | solution.py:129
  83.1 2.5 convolution_bitcast_fusion.1
  91.5 31.9 %psum.14 = f32[]{:T(128)} all-reduce(f32[]{:T(128)S(6)} %sub.109), channel_id=1, replica_groups=mesh['groups'=2,'seq'=16] {'seq'}, use_global_device_ids=true, to_apply=%region_6.7 | all-reduce | flops 1 | bytes 8 | tf_op jit(solution)/shard_map/psum | solution.py:91
  123.4 1.8 slice.98
  125.2 1.9 slice.77
  127.1 4.7 %convolution_bitcast_fusion.4 = f32[192,8,128]{2,0,1:T(8,128)S(1)} fusion(f32[8,64,192]{2,1,0:T(8,128)} %fusion.44, bf16[64,8,128]{2,1,0:T(8,128)(2,1)S(1)} %bitcast.112, f32[8,64,192]{2,1,0:T(8,128)} %get-tuple-element.19, f32[8,64]{1,0:T(8,128)S(1)} %get-tuple-element.18), kind=kOutput, calls=%fused_computation.13 | convolution fusion | flops 25854656 | bytes 1705984 | tf_op jit(solution)/shard_map/hqk,qhd->khd/dot_general | solution.py:126
  132.3 2.1 fusion.39
  134.4 4.8 %convolution_bitcast_fusion.3 = f32[192,8,128]{2,0,1:T(8,128)S(1)} fusion(f32[8,64,192]{2,1,0:T(8,128)} %fusion.39, bf16[64,8,128]{2,1,0:T(8,128)(2,1)} %bitcast.110, f32[8,64,192]{2,1,0:T(8,128)} %get-tuple-element.21, f32[8,64]{1,0:T(8,128)S(1)} %copy-done.18), kind=kOutput, calls=%fused_computation.12 | convolution fusion | flops 25854656 | bytes 1705984 | tf_op jit(solution)/shard_map/hqk,qhd->khd/dot_general | solution.py:126
  144.1 4.1 %fusion.25 = bf16[64,8,128]{2,0,1:T(8,128)(2,1)S(1)} fusion(f32[8,64,192]{2,1,0:T(8,128)} %fusion.44, bf16[192,8,128]{2,1,0:T(8,128)(2,1)S(1)} %bitcast.108, f32[8,64,192]{2,1,0:T(8,128)} %get-tuple-element.19, f32[8,64]{1,0:T(8,128)S(1)} %get-tuple-element.18), kind=kOutput, calls=%fused_computation.38 | convolution fusion | flops 25920192 | bytes 1312768 | tf_op jit(solution)/shard_map/hqk,khd->qhd/dot_general | solution.py:117
  151.7 4.2 %fusion.26 = bf16[64,8,128]{2,0,1:T(8,128)(2,1)S(1)} fusion(f32[8,64,192]{2,1,0:T(8,128)} %fusion.39, bf16[192,8,128]{2,1,0:T(8,128)(2,1)S(1)} %bitcast.106, f32[8,64,192]{2,1,0:T(8,128)} %get-tuple-element.21, f32[8,64]{1,0:T(8,128)S(1)} %copy-done.18), kind=kOutput, calls=%fused_computation.39 | convolution fusion | flops 25920192 | bytes 1312768 | tf_op jit(solution)/shard_map/hqk,khd->qhd/dot_general | solution.py:117
  156.1 4.5 %collective-permute-start.6 = (bf16[2,64,1024]{2,1,0:T(8,128)(2,1)}, bf16[2,64,1024]{2,1,0:T(8,128)(2,1)S(1)}, u32[]{:S(2)}, u32[]{:S(2)}) collective-permute-start(bf16[2,64,1024]{2,1,0:T(8,128)(2,1)} %slice.99), channel_id=1, source_target_pairs={{0,15},{1,0},{2,1},{3,2},{4,3},{5,4},{6,5},{7,6},{8,7},{9,8},{10,9... | collective-permute-start | bytes 786440 | tf_op jit(solution)/shard_map/ppermute | solution.py:11
  162.0 1.9 fusion.36
  165.1 5.6 %collective-permute-done.7 = f32[2,64,1024]{2,1,0:T(8,128)S(1)} collective-permute-done((f32[2,64,1024]{2,1,0:T(8,128)}, f32[2,64,1024]{2,1,0:T(8,128)S(1)}, u32[]{:S(2)}, u32[]{:S(2)}) %collective-permute-start.7) | collective-permute-done | bytes 524320 | tf_op jit(solution)/shard_map/ppermute | solution.py:11
  170.7 1.8 fusion.38
  172.6 2.7 %fusion.92 = f32[64,2048]{1,0:T(8,128)} fusion(f32[64,256]{1,0:T(8,128)} %reduce-scatter.2.cloned.1.call-done, bf16[2048,256]{1,0:T(8,128)(2,1)S(1)} %copy-done), kind=kOutput, calls=%fused_computation.145 | convolution fusion | flops 402653184 | bytes 1638400 | tf_op jit(solution)/shard_map/dot_general | solution.py:102
  175.3 77.2 %all-reduce.2.cloned.1.call-done = f32[2048,256]{1,0:T(8,128)} async-done(((f32[2048,256]{1,0:T(8,128)}), f32[2048,256]{1,0:T(8,128)}) %all-reduce.2.cloned.1.call-update) | async-done | bytes 2097168 | tf_op jit(solution)/shard_map/psum | solution.py:91
  252.5 3.0 %copy.122 = f32[2048,256]{1,0:T(8,128)} copy(f32[2048,256]{1,0:T(8,128)} %all-reduce.2.cloned.1.call-done) | data formatting | bytes 4194304
  (118 shorter events, 35.3 us)
Async XLA Ops:
  7.2 61.7 %copy-start = (bf16[2048,256]{1,0:T(8,128)(2,1)S(1)}, bf16[2048,256]{1,0:T(8,128)(2,1)}, u32[]{:S(2)}) copy-start(bf16[2048,256]{1,0:T(8,128)(2,1)} %param.13) | copy-start | bytes 3145732
  7.2 21.6 %copy-start.11 = (bf16[2,64,1024]{2,1,0:T(8,128)(2,1)S(1)}, bf16[2,64,1024]{2,1,0:T(8,128)(2,1)}, u32[]{:S(2)}) copy-start(bf16[2,64,1024]{2,1,0:T(8,128)(2,1)} %param.10) | copy-start | bytes 786436
  7.2 58.7 %all-gather.2.cloned.1.call-start = ((), (), s32[]{:S(2)}) async-start(), calls=%async_computation.1 | async-start | bytes 4456448 | tf_op jit(solution)/shard_map/all_gather | solution.py:80
  7.9 164.6 %reduce-scatter.2.cloned.1.call-start = ((), (), s32[]{:S(2)}) async-start(), calls=%async_computation.2 | async-start | bytes 1114112 | tf_op jit(solution)/shard_map/reduce_scatter | solution.py:96
  8.6 11.6 %collective-permute-start.3 = (bf16[64]{0:T(256)(128)(2,1)S(1)}, bf16[64]{0:T(256)(128)(2,1)S(1)}, u32[]{:S(2)}, u32[]{:S(2)}) collective-permute-start(bf16[64]{0:T(256)(128)(2,1)S(1)} %convert_element_type.83), channel_id=1, source_target_pairs={{0,15},{1,0},{2,1},{3,2},{4,3},{5,4},{6,5},{7,6},{8,7},{9,8},{10,9... | collective-permute-start | bytes 392 | tf_op jit(solution)/shard_map/ppermute | solution.py:11
  14.1 10.6 %collective-permute-start.2 = (bf16[64]{0:T(256)(128)(2,1)S(1)}, bf16[64]{0:T(256)(128)(2,1)S(1)}, u32[]{:S(2)}, u32[]{:S(2)}) collective-permute-start(bf16[64]{0:T(256)(128)(2,1)S(1)} %convert_element_type.83), channel_id=1, source_target_pairs={{0,1},{1,2},{2,3},{3,4},{4,5},{5,6},{6,7},{7,8},{8,9},{9,10},{10,1... | collective-permute-start | bytes 392 | tf_op jit(solution)/shard_map/ppermute | solution.py:11
  14.1 15.9 %collective-permute-start.4 = (bf16[2,64,1024]{2,1,0:T(8,128)(2,1)}, bf16[2,64,1024]{2,1,0:T(8,128)(2,1)S(1)}, u32[]{:S(2)}, u32[]{:S(2)}) collective-permute-start(bf16[2,64,1024]{2,1,0:T(8,128)(2,1)} %param.9), channel_id=1, source_target_pairs={{0,1},{1,2},{2,3},{3,4},{4,5},{5,6},{6,7},{7,8},{8,9},{9,10},{10,1... | collective-permute-start | bytes 786440 | tf_op jit(solution)/shard_map/ppermute | solution.py:11
  14.1 16.7 %collective-permute-start.5 = (bf16[2,64,1024]{2,1,0:T(8,128)(2,1)}, bf16[2,64,1024]{2,1,0:T(8,128)(2,1)S(1)}, u32[]{:S(2)}, u32[]{:S(2)}) collective-permute-start(bf16[2,64,1024]{2,1,0:T(8,128)(2,1)} %param.9), channel_id=1, source_target_pairs={{0,15},{1,0},{2,1},{3,2},{4,3},{5,4},{6,5},{7,6},{8,7},{9,8},{10,9... | collective-permute-start | bytes 786440 | tf_op jit(solution)/shard_map/ppermute | solution.py:11
  18.6 10.2 %collective-permute-start = (bf16[2,64,1024]{2,1,0:T(8,128)(2,1)}, bf16[2,64,1024]{2,1,0:T(8,128)(2,1)S(1)}, u32[]{:S(2)}, u32[]{:S(2)}) collective-permute-start(bf16[2,64,1024]{2,1,0:T(8,128)(2,1)} %param.10), channel_id=1, source_target_pairs={{0,1},{1,2},{2,3},{3,4},{4,5},{5,6},{6,7},{7,8},{8,9},{9,10},{10,1... | collective-permute-start | bytes 786440 | tf_op jit(solution)/shard_map/ppermute | solution.py:11
  19.6 11.5 %copy-start.14 = (bf16[8,8,8,128]{3,2,1,0:T(8,128)(2,1)}, bf16[8,8,8,128]{3,2,1,0:T(8,128)(2,1)S(1)}, u32[]{:S(2)}) copy-start(bf16[8,8,8,128]{3,2,1,0:T(8,128)(2,1)S(1)} %copy.72) | copy-start | bytes 393220
  20.3 9.5 %collective-permute-start.1 = (bf16[2,64,1024]{2,1,0:T(8,128)(2,1)}, bf16[2,64,1024]{2,1,0:T(8,128)(2,1)S(1)}, u32[]{:S(2)}, u32[]{:S(2)}) collective-permute-start(bf16[2,64,1024]{2,1,0:T(8,128)(2,1)} %param.10), channel_id=1, source_target_pairs={{0,15},{1,0},{2,1},{3,2},{4,3},{5,4},{6,5},{7,6},{8,7},{9,8},{10,9... | collective-permute-start | bytes 786440 | tf_op jit(solution)/shard_map/ppermute | solution.py:11
  31.0 3.8 %copy-start.9 = (bf16[24,8,8,128]{3,2,1,0:T(8,128)(2,1)}, bf16[24,8,8,128]{3,2,1,0:T(8,128)(2,1)S(1)}, u32[]{:S(2)}) copy-start(bf16[24,8,8,128]{3,2,1,0:T(8,128)(2,1)S(1)} %copy.68) | copy-start | bytes 1179652
  32.1 2.6 copy-start.5
  35.2 1.9 copy-start.6
  70.7 4.1 %copy-start.2 = (bf16[128,256]{1,0:T(8,128)(2,1)}, bf16[128,256]{1,0:T(8,128)(2,1)S(1)}, u32[]{:S(2)}) copy-start(bf16[128,256]{1,0:T(8,128)(2,1)S(1)} %get-tuple-element.16) | copy-start | bytes 196612
  88.2 164.3 %all-reduce.2.cloned.1.call-start = ((), (), s32[]{:S(2)}) async-start(), calls=%async_computation.3 | async-start | bytes 4194304 | tf_op jit(solution)/shard_map/psum | solution.py:91
  90.5 36.6 %copy-start.16 = (bf16[8,8,8,128]{3,2,1,0:T(8,128)(2,1)S(1)}, bf16[8,8,8,128]{3,2,1,0:T(8,128)(2,1)}, u32[]{:S(2)}) copy-start(bf16[8,8,8,128]{3,2,1,0:T(8,128)(2,1)} %copy.69) | copy-start | bytes 393220
  141.9 2.2 copy-start.10
  144.1 4.4 %copy-start.4 = (f32[2,64,1024]{2,1,0:T(8,128)S(1)}, f32[2,64,1024]{2,1,0:T(8,128)}, u32[]{:S(2)}) copy-start(f32[2,64,1024]{2,1,0:T(8,128)} %slice.77) | copy-start | bytes 1572868
  144.1 4.9 %copy-start.3 = (bf16[128,256]{1,0:T(8,128)(2,1)S(1)}, bf16[128,256]{1,0:T(8,128)(2,1)}, u32[]{:S(2)}) copy-start(bf16[128,256]{1,0:T(8,128)(2,1)} %copy-done.2) | copy-start | bytes 196612
  148.4 13.6 %collective-permute-start.8 = (bf16[2,64,1024]{2,1,0:T(8,128)(2,1)}, bf16[2,64,1024]{2,1,0:T(8,128)(2,1)}, u32[]{:S(2)}, u32[]{:S(2)}) collective-permute-start(bf16[2,64,1024]{2,1,0:T(8,128)(2,1)} %slice.98), channel_id=1, source_target_pairs={{0,15},{1,0},{2,1},{3,2},{4,3},{5,4},{6,5},{7,6},{8,7},{9,8},{10,9... | collective-permute-start | bytes 786440 | tf_op jit(solution)/shard_map/ppermute | solution.py:11
  148.5 13.5 %collective-permute-start.9 = (f32[2,64,1024]{2,1,0:T(8,128)S(1)}, f32[2,64,1024]{2,1,0:T(8,128)S(1)}, u32[]{:S(2)}, u32[]{:S(2)}) collective-permute-start(f32[2,64,1024]{2,1,0:T(8,128)S(1)} %copy-done.4), channel_id=1, source_target_pairs={{0,1},{1,2},{2,3},{3,4},{4,5},{5,6},{6,7},{7,8},{8,9},{9,10},{10,1... | collective-permute-start | bytes 1572872 | tf_op jit(solution)/shard_map/ppermute | solution.py:11
  149.0 21.7 %collective-permute-start.7 = (f32[2,64,1024]{2,1,0:T(8,128)}, f32[2,64,1024]{2,1,0:T(8,128)S(1)}, u32[]{:S(2)}, u32[]{:S(2)}) collective-permute-start(f32[2,64,1024]{2,1,0:T(8,128)} %slice.74), channel_id=1, source_target_pairs={{0,1},{1,2},{2,3},{3,4},{4,5},{5,6},{6,7},{7,8},{8,9},{9,10},{10,1... | collective-permute-start | bytes 1572872 | tf_op jit(solution)/shard_map/ppermute | solution.py:11
  156.1 9.0 %collective-permute-start.6 = (bf16[2,64,1024]{2,1,0:T(8,128)(2,1)}, bf16[2,64,1024]{2,1,0:T(8,128)(2,1)S(1)}, u32[]{:S(2)}, u32[]{:S(2)}) collective-permute-start(bf16[2,64,1024]{2,1,0:T(8,128)(2,1)} %slice.99), channel_id=1, source_target_pairs={{0,15},{1,0},{2,1},{3,2},{4,3},{5,4},{6,5},{7,6},{8,7},{9,8},{10,9... | collective-permute-start | bytes 786440 | tf_op jit(solution)/shard_map/ppermute | solution.py:11
  (8 other events, 8.5 us)
Sparse Core Ops, SparseCore 0:
  10.2 55.6 all-gather.1
  88.3 55.9 reduce-scatter.1
  150.9 101.5 all-reduce.1
where the time goes:
time: 264 us; the launch traced here: 263 us
  waiting for transfers between devices  117 us (44%)
  matrix products  42.8 us (16%)
  blocking collectives  31.9 us (12%)
  local copies, waits for them, and re-layouts  24.8 us (9%)
  starting transfers between devices  19.5 us (7%)
  between operations  17.4 us (7%)
  other arithmetic  10.1 us (4%)
    psum x1, waiting for transfers between devices, per_device(): score_total, d_w_head = lax.psum((crps_sum, head_local), 'seq')  77.2 us
    psum x1, blocking collectives, per_device(): score_total, d_w_head = lax.psum((crps_sum, head_local), 'seq')  31.9 us
    all_gather x1, waiting for transfers between devices, per_device(): whole_out = lax.all_gather(w_out, 'seq', axis=0, tiled=True)  28.5 us
    ppermute x10, starting transfers between devices, passed_along(): return lax.ppermute(x, axis, [(i, (i + by) % peers) for i in range(peers)])  19.4 us
    unnamed x56, local copies, waits for them, and re-layouts  10.4 us
    ppermute x10, waiting for transfers between devices, passed_along(): return lax.ppermute(x, axis, [(i, (i + by) % peers) for i in range(peers)])  10.3 us
    dot_general x2, matrix products, per_device(): jnp.einsum('hqk,qhd->khd', d_scores, query_heads, preferred_element_type=...  9.48 us
    dot_general x2, matrix products, per_device(): jnp.einsum('hqk,khd->qhd', d_scores, split_heads(window_keys[member]), pr...  8.29 us
  transfers between devices with their start and end apart: 13, of which 6 were waited for; matrix products, arithmetic and copies ran while one was open for 19% of the time, Pallas kernels for 0%

commit v1 on v0

v1 whole, which is shorter than its diff:
```python
import functools

import jax
import jax.numpy as jnp
from jax import lax
from jax.experimental import pallas as pl
from jax.experimental.pallas import tpu as pltpu
from jax.sharding import PartitionSpec as P

DH = 128
F32 = jnp.float32
BF16 = jnp.bfloat16


def dot_nn(a, b):
    return lax.dot_general(a, b, (((1,), (0,)), ((), ())), preferred_element_type=F32)


def dot_nt(a, b, precision=None):
    return lax.dot_general(
        a, b, (((1,), (1,)), ((), ())), preferred_element_type=F32, precision=precision
    )


def dot_tn(a, b):
    return lax.dot_general(a, b, (((0,), (0,)), ((), ())), preferred_element_type=F32)


def kernel(
    n,
    q, k, v, resid, w_out, w_head, target, ids,
    loss_o, dq_o, dk_o, dv_o, dwo_o, dwh_o,
    kw, vw, qw, idw, dpw, stw,
    m_all, pred0, bias, probs, att, dpred, da, stats, stats_t,
    ap_f, ap_b, ap_r1, ap_s2, ap_r2,
    g_f, g_b, g_r1, g_s2, g_r2,
    loss_own, loss_sib, loss_all,
    halo_ss, halo_rs, m_ss, m_rs, sib_ss, sib_rs, ap_ss, ap_rs, g_ss, g_rs,
    ag_ss, ag_rs, fw_ss, fw_rs, lo_ss, lo_rs,
):
    members, tok, hd = q.shape
    heads = hd // DH
    dm = resid.shape[2]
    nc = n // 2
    ar = hd // n
    gr = dm // n
    scaling = DH ** (-0.5)
    me = lax.axis_index("seq")
    chip, par = me // 2, me % 2
    sib = chip * 2 + (1 - par)
    left, right = lax.rem(me + n - 1, n), lax.rem(me + 1, n)
    outer = lax.rem(me + n - 1 + 2 * par, n)

    def peer_chip(off):
        return lax.rem(chip + off, nc)

    def source_chip(off):
        return lax.rem(chip + nc - off, nc)

    def remote(src, dst, ss, rs, to):
        copy = pltpu.make_async_remote_copy(
            src_ref=src, dst_ref=dst, send_sem=ss, recv_sem=rs,
            device_id={"seq": to}, device_id_type=pl.DeviceIdType.MESH,
        )
        copy.start()
        return copy

    barrier = pltpu.get_barrier_semaphore()
    for to in [sib, outer] + [peer_chip(off) * 2 + par for off in range(1, nc)]:
        pl.semaphore_signal(
            barrier, inc=1, device_id={"seq": to}, device_id_type=pl.DeviceIdType.MESH
        )
    pl.semaphore_wait(barrier, nc + 1)

    pending = []

    def halo(slot, src, dst):
        pair = (
            remote(src, dst.at[0], halo_ss.at[2 * slot], halo_rs.at[2 * slot], right),
            remote(src, dst.at[1], halo_ss.at[2 * slot + 1], halo_rs.at[2 * slot + 1], left),
        )
        pending.extend(pair)
        return pair

    halo_id = halo(0, ids, idw)
    halo_k = halo(1, k, kw)
    halo_v = halo(2, v, vw)

    m_all[chip, par] = dot_nn(w_out[...], w_head[...]).astype(BF16)
    m_copies = [
        remote(m_all.at[chip, par], m_all.at[chip, par], m_ss.at[off], m_rs.at[off],
               peer_chip(off) * 2 + par)
        for off in range(1, nc)
    ]
    pending.extend(m_copies)
    halo_q = halo(3, q, qw)

    pred0[...] = dot_nn(resid[...].reshape(members * tok, dm), w_head[...])

    for copy in halo_id + halo_k:
        copy.wait_recv()
    id_window = jnp.concatenate([idw[0], ids[...], idw[1]], axis=0)
    lane = lax.broadcasted_iota(jnp.int32, (tok, DH), 1)
    first = jnp.where(lane == 0, 1.0, 0.0).astype(BF16)
    window_ids = dot_nt(first, id_window)
    own_ids = ids[...].astype(F32)[:, 0:1]
    gap = jnp.abs(own_ids - window_ids)
    number = 4.0 * n
    bias[...] = jnp.where((gap < 1.5) | (gap > number - 1.5), 0.0, -1e30)

    def cols(h):
        return pl.ds(pl.multiple_of(h * DH, DH), DH)

    def window(side, own, m, h):
        return jnp.concatenate(
            [side[0, m, :, cols(h)], own[m, :, cols(h)], side[1, m, :, cols(h)]], axis=0
        )

    unroll = 2

    def softmax_step(step, held):
        for u in range(unroll):
            h = step * unroll + u
            for m in range(members):
                c = m * heads + h
                s = dot_nt(q[m, :, cols(h)], window(kw, k, m, h)) * scaling + bias[...]
                peak = jnp.max(s, axis=-1, keepdims=True)
                e = jnp.exp(s - peak)
                total = jnp.sum(e, axis=-1, keepdims=True)
                probs[c] = e / total
                held = jnp.where(lane == c, peak + jnp.log(total), held)
        return held

    lse = lax.fori_loop(0, heads // unroll, softmax_step, jnp.zeros((tok, DH), F32))

    for copy in m_copies:
        copy.wait_recv()
    m_forward = remote(m_all.at[:, par], m_all.at[:, par], sib_ss.at[0], sib_rs.at[0], sib)
    pending.append(m_forward)
    for copy in halo_v:
        copy.wait_recv()

    def attend_step(step, _):
        for u in range(unroll):
            h = step * unroll + u
            for m in range(members):
                p = probs[m * heads + h].astype(BF16)
                att[m, :, cols(h)] = dot_nn(p, window(vw, v, m, h)).astype(BF16)
        return 0

    lax.fori_loop(0, heads // unroll, attend_step, 0)

    m_forward.wait_recv()
    attended = att[...].reshape(members * tok, hd)
    m_full = m_all[...].reshape(hd, -1)
    predicted = pred0[...] + dot_nn(attended, m_full)
    p0, p1 = predicted[:tok], predicted[tok:]
    o0, o1, pair = p0 - target[...], p1 - target[...], p0 - p1
    s0 = jnp.sqrt(1.0 + o0 * o0)
    s1 = jnp.sqrt(1.0 + o1 * o1)
    sp = jnp.sqrt(1.0 + pair * pair)
    score = 0.5 * ((s0 - 1.0) + (s1 - 1.0)) - 0.5 * (sp - 1.0)
    shared = 0.5 * (pair / sp)
    dpred[0:tok] = (0.5 * (o0 / s0) - shared).astype(BF16)
    dpred[tok:] = (0.5 * (o1 / s1) + shared).astype(BF16)
    halo_d = halo(4, dpred, dpw)

    step_rows = 256
    per = step_rows // (2 * ar)
    for i in range(hd // step_rows):
        part = dot_tn(attended[:, i * step_rows:(i + 1) * step_rows], dpred[...])
        part = part.reshape(per, 2, ar, -1)
        ap_f[i * per:(i + 1) * per] = part
        ap_b[i * per:(i + 1) * per] = part.astype(BF16)
    ap_pair = remote(ap_b.at[:, 1 - par], ap_r1, sib_ss.at[1], sib_rs.at[1], sib)
    pending.append(ap_pair)

    loss_own[...] = jnp.broadcast_to(jnp.sum(score).reshape(1, 1), loss_own.shape)
    loss_pair = remote(loss_own, loss_sib, sib_ss.at[2], sib_rs.at[2], sib)
    pending.append(loss_pair)

    da[1] = dot_nt(dpred[...], m_full).astype(BF16).reshape(members, tok, hd)

    ap_pair.wait_recv()
    ap_copies = []
    for off in range(1, nc):
        c = peer_chip(off)
        ap_s2[c] = (ap_f[c, par] + ap_r1[c].astype(F32)).astype(BF16)
        ap_copies.append(
            remote(ap_s2.at[c], ap_r2.at[off], ap_ss.at[off], ap_rs.at[off], c * 2 + par)
        )
    pending.extend(ap_copies)
    loss_pair.wait_recv()
    loss_all[chip] = loss_own[...] + loss_sib[...]
    loss_copies = [
        remote(loss_all.at[chip], loss_all.at[chip], lo_ss.at[off], lo_rs.at[off],
               peer_chip(off) * 2 + par)
        for off in range(1, nc)
    ]
    pending.extend(loss_copies)

    gper = step_rows // (2 * gr)
    rows = resid[...].reshape(members * tok, dm)
    for i in range(dm // step_rows):
        part = dot_tn(rows[:, i * step_rows:(i + 1) * step_rows], dpred[...])
        g_f[i * gper:(i + 1) * gper] = part.reshape(gper, 2, gr, -1)

    def query_grad_step(step, held):
        for u in range(unroll):
            h = step * unroll + u
            for m in range(members):
                c = m * heads + h
                p = probs[c]
                dp = dot_nt(da[1, m, :, cols(h)], window(vw, v, m, h))
                delta = jnp.sum(p * dp, axis=-1, keepdims=True)
                ds = (p * (dp - delta) * scaling).astype(BF16)
                dq_o[m, :, cols(h)] = dot_nn(ds, window(kw, k, m, h)).astype(BF16)
                held = jnp.where(lane == members * heads + c, delta, held)
        return held

    stats[...] = lax.fori_loop(0, heads // unroll, query_grad_step, lse)
    halo_s = halo(5, stats, stw)

    for copy in ap_copies:
        copy.wait_recv()
    ap_total = ap_f[chip, par] + ap_r1[chip].astype(F32)
    for off in range(1, nc):
        ap_total = ap_total + ap_r2[off].astype(F32)
    ap_high = ap_total.astype(BF16)
    for i in range(dm // step_rows):
        part = dot_tn(w_out[:, i * step_rows:(i + 1) * step_rows], ap_high)
        part = g_f[i * gper:(i + 1) * gper] + part.reshape(gper, 2, gr, -1)
        g_f[i * gper:(i + 1) * gper] = part
        g_b[i * gper:(i + 1) * gper] = part.astype(BF16)
    g_pair = remote(g_b.at[:, 1 - par], g_r1, sib_ss.at[3], sib_rs.at[3], sib)
    pending.append(g_pair)
    ap_low = (ap_total - ap_high.astype(F32)).astype(BF16)
    dwo_o[...] = dot_nt(ap_high, w_head[...]) + dot_nt(ap_low, w_head[...])
    g_pair.wait_recv()
    g_copies = []
    for off in range(1, nc):
        c = peer_chip(off)
        g_s2[c] = (g_f[c, par] + g_r1[c].astype(F32)).astype(BF16)
        g_copies.append(
            remote(g_s2.at[c], g_r2.at[off], g_ss.at[off], g_rs.at[off], c * 2 + par)
        )
    pending.extend(g_copies)

    for copy in halo_d:
        copy.wait_recv()
    for side, place in ((0, 0), (1, 2)):
        da[place] = dot_nt(dpw[side], m_full).astype(BF16).reshape(members, tok, hd)
    for copy in halo_q + halo_s:
        copy.wait_recv()
    stat_window = jnp.concatenate([stw[0], stats[...], stw[1]], axis=0)
    count = stats_t.shape[0]
    eye = jnp.where(
        lax.broadcasted_iota(jnp.int32, (count, DH), 0)
        == lax.broadcasted_iota(jnp.int32, (count, DH), 1), 1.0, 0.0
    )
    stats_t[...] = dot_nt(eye, stat_window, lax.Precision.HIGHEST)

    def key_grad_step(step, _):
        for u in range(unroll):
            h = step * unroll + u
            for m in range(members):
                c = m * heads + h
                queries = window(qw, q, m, h)
                grads = jnp.concatenate([da[i, m, :, cols(h)] for i in range(3)], axis=0)
                s = dot_nt(k[m, :, cols(h)], queries) * scaling + bias[...]
                p = jnp.exp(s - stats_t[pl.ds(c, 1), :])
                dp = dot_nt(v[m, :, cols(h)], grads)
                ds = (p * (dp - stats_t[pl.ds(members * heads + c, 1), :]) * scaling).astype(BF16)
                dv_o[m, :, cols(h)] = dot_nn(p.astype(BF16), grads).astype(BF16)
                dk_o[m, :, cols(h)] = dot_nn(ds, queries).astype(BF16)
        return 0

    lax.fori_loop(0, heads // unroll, key_grad_step, 0)

    for copy in g_copies:
        copy.wait_recv()
    g_total = g_f[chip, par] + g_r1[chip].astype(F32)
    for off in range(1, nc):
        g_total = g_total + g_r2[off].astype(F32)
    dwh_o[chip, par] = g_total.astype(BF16)
    ag_copies = [
        remote(dwh_o.at[chip, par], dwh_o.at[chip, par], ag_ss.at[off], ag_rs.at[off],
               peer_chip(off) * 2 + par)
        for off in range(1, nc)
    ]
    pending.extend(ag_copies)
    forwards = [remote(dwh_o.at[chip, par], dwh_o.at[chip, par], fw_ss.at[0], fw_rs.at[0], sib)]
    for copy in loss_copies:
        copy.wait_recv()
    loss_o[...] = jnp.sum(loss_all[...], axis=0)
    for off in range(1, nc):
        ag_copies[off - 1].wait_recv()
        c = source_chip(off)
        forwards.append(
            remote(dwh_o.at[c, par], dwh_o.at[c, par], fw_ss.at[off], fw_rs.at[off], sib)
        )
    for copy in forwards:
        copy.wait_recv()
    for copy in pending + forwards:
        copy.wait_send()


def per_device(queries, keys, values, resid, w_out, w_head, target, block_ids):
    members, tok, hd = queries.shape
    heads = hd // DH
    n = lax.axis_size("seq")
    nc = n // 2
    dm, width = w_head.shape
    ar, gr = hd // n, dm // n
    ids = jnp.broadcast_to(block_ids.astype(BF16)[:, None], (tok, DH))
    vm = pl.BlockSpec(memory_space=pltpu.VMEM)
    dma = pltpu.SemaphoreType.DMA
    like = jax.ShapeDtypeStruct(queries.shape, BF16)
    loss, d_queries, d_keys, d_values, d_w_out, d_w_head = pl.pallas_call(
        functools.partial(kernel, n),
        out_shape=(
            jax.ShapeDtypeStruct((8, DH), F32),
            like, like, like,
            jax.ShapeDtypeStruct((ar, dm), F32),
            jax.ShapeDtypeStruct((nc, 2, gr, width), BF16),
        ),
        in_specs=[vm] * 8,
        out_specs=(vm,) * 6,
        scratch_shapes=[
            pltpu.VMEM((2,) + keys.shape, BF16),
            pltpu.VMEM((2,) + keys.shape, BF16),
            pltpu.VMEM((2,) + keys.shape, BF16),
            pltpu.VMEM((2, tok, DH), BF16),
            pltpu.VMEM((2, members * tok, width), BF16),
            pltpu.VMEM((2, tok, DH), F32),
            pltpu.VMEM((nc, 2, ar, width), BF16),
            pltpu.VMEM((members * tok, width), F32),
            pltpu.VMEM((tok, 3 * tok), F32),
            pltpu.VMEM((members * heads, tok, 3 * tok), F32),
            pltpu.VMEM(queries.shape, BF16),
            pltpu.VMEM((members * tok, width), BF16),
            pltpu.VMEM((3,) + queries.shape, BF16),
            pltpu.VMEM((tok, DH), F32),
            pltpu.VMEM((2 * members * heads, 3 * tok), F32),
            pltpu.VMEM((nc, 2, ar, width), F32),
            pltpu.VMEM((nc, 2, ar, width), BF16),
            pltpu.VMEM((nc, ar, width), BF16),
            pltpu.VMEM((nc, ar, width), BF16),
            pltpu.VMEM((nc, ar, width), BF16),
            pltpu.VMEM((nc, 2, gr, width), F32),
            pltpu.VMEM((nc, 2, gr, width), BF16),
            pltpu.VMEM((nc, gr, width), BF16),
            pltpu.VMEM((nc, gr, width), BF16),
            pltpu.VMEM((nc, gr, width), BF16),
            pltpu.VMEM((8, DH), F32),
            pltpu.VMEM((8, DH), F32),
            pltpu.VMEM((nc, 8, DH), F32),
            dma((12,)), dma((12,)),
            dma((nc,)), dma((nc,)),
            dma((4,)), dma((4,)),
            dma((nc,)), dma((nc,)),
            dma((nc,)), dma((nc,)),
            dma((nc,)), dma((nc,)),
            dma((nc,)), dma((nc,)),
            dma((nc,)), dma((nc,)),
        ],
        compiler_params=pltpu.CompilerParams(
            collective_id=0, has_side_effects=True, vmem_limit_bytes=48 * 1024 * 1024
        ),
        cost_estimate=pl.CostEstimate(
            flops=2_000_000_000, bytes_accessed=6_000_000, transcendentals=1_000_000
        ),
    )(queries, keys, values, resid, w_out, w_head, target, ids)
    loss = (loss[0, 0] / (n * tok * width)).reshape(1)
    return (
        loss, d_queries, d_keys, d_values, d_w_out,
        d_w_head.reshape(dm, width).astype(F32),
    )


def solution(mesh):
    return jax.shard_map(
        per_device,
        mesh=mesh,
        in_specs=(
            P("groups", "seq", None),
            P("groups", "seq", None),
            P("groups", "seq", None),
            P("groups", "seq", None),
            P("seq", None),
            P(),
            P(("groups", "seq"), None),
            P(("groups", "seq")),
        ),
        out_specs=(
            P("groups"),
            P("groups", "seq", None),
            P("groups", "seq", None),
            P("groups", "seq", None),
            P(("groups", "seq"), None),
            P("groups", None),
        ),
        check_vma=False,
    )
```

time: 264 us -> 78.4 us (0.30)
  the two profiles are of different devices: /device:TPU:0 before, /device:TPU:27 now
where the time goes in v1:
time: 78.4 us; the launch traced here: 78 us
  Pallas kernels  63 us (80%)
  local copies, waits for them, and re-layouts  10.4 us (13%)
  between operations  2.43 us (3%)
  other arithmetic  2.21 us (3%)
    pallas_call x1, Pallas kernels, per_device(): pl.pallas_call(functools.partial(kernel, n), out_shape=(jax.ShapeDtypeStr...  63 us
    unnamed x18, local copies, waits for them, and re-layouts  9.81 us

profile of v1, /device:TPU:27, one launch (start us, length us, event | category | flops | bytes accessed | tf_op | source)
XLA Modules:
  0.0 78.0 jit_solution(13130453856080842930)
XLA Ops:
  0.6 0.7 convert_element_type.9
  1.3 0.1 broadcast_in_dim.2.ids
  1.4 0.0 copy-start
  1.4 1.2 %copy-done = bf16[2048,256]{1,0:T(8,128)(2,1)S(1)} copy-done((bf16[2048,256]{1,0:T(8,128)(2,1)S(1)}, bf16[2048,256]{1,0:T(8,128)(2,1)}, u32[]{:S(2)}) %copy-start) | copy-done | bytes 1048600
  2.6 0.0 copy-start.1
  2.6 1.0 %copy-done.1 = bf16[2,64,2048]{2,1,0:T(8,128)(2,1)S(1)} copy-done((bf16[2,64,2048]{2,1,0:T(8,128)(2,1)S(1)}, bf16[2,64,2048]{2,1,0:T(8,128)(2,1)}, u32[]{:S(2)}) %copy-start.1) | copy-done | bytes 524312
  3.6 0.0 copy-start.2
  3.6 0.9 %copy-done.2 = bf16[2,64,1024]{2,1,0:T(8,128)(2,1)S(1)} copy-done((bf16[2,64,1024]{2,1,0:T(8,128)(2,1)S(1)}, bf16[2,64,1024]{2,1,0:T(8,128)(2,1)}, u32[]{:S(2)}) %copy-start.2) | copy-done | bytes 262168
  4.6 0.0 copy-start.3
  4.6 0.9 %copy-done.3 = bf16[2,64,1024]{2,1,0:T(8,128)(2,1)S(1)} copy-done((bf16[2,64,1024]{2,1,0:T(8,128)(2,1)S(1)}, bf16[2,64,1024]{2,1,0:T(8,128)(2,1)}, u32[]{:S(2)}) %copy-start.3) | copy-done | bytes 262168
  5.5 0.0 copy-start.4
  5.5 0.9 %copy-done.4 = bf16[2,64,1024]{2,1,0:T(8,128)(2,1)S(1)} copy-done((bf16[2,64,1024]{2,1,0:T(8,128)(2,1)S(1)}, bf16[2,64,1024]{2,1,0:T(8,128)(2,1)}, u32[]{:S(2)}) %copy-start.4) | copy-done | bytes 262168
  6.5 0.0 copy-start.5
  6.5 0.9 %copy-done.5 = bf16[64,2048]{1,0:T(8,128)(2,1)S(1)} copy-done((bf16[64,2048]{1,0:T(8,128)(2,1)S(1)}, bf16[64,2048]{1,0:T(8,128)(2,1)}, u32[]{:S(2)}) %copy-start.5) | copy-done | bytes 262168
  7.4 0.0 copy-start.6
  7.4 0.8 %copy-done.6 = f32[64,256]{1,0:T(8,128)S(1)} copy-done((f32[64,256]{1,0:T(8,128)S(1)}, f32[64,256]{1,0:T(8,128)}, u32[]{:S(2)}) %copy-start.6) | copy-done | bytes 65560
  8.3 63.0 %shard_map.127 = (f32[8,128]{1,0:T(8,128)S(1)}, bf16[2,64,1024]{2,1,0:T(8,128)(2,1)S(1)}, bf16[2,64,1024]{2,1,0:T(8,128)(2,1)S(1)}, bf16[2,64,1024]{2,1,0:T(8,12...) custom-call(bf16[2,64,1024]{2,1,0:T(8,128)(2,1)S(1)} %copy-done.2, ...), custom_call_target="tpu_custom_call" | custom-call | flops 2000000000 | bytes 6000000 | tf_op jit(solution)/shard_map/pallas_call | solution.py:319
  71.3 0.5 slice.3
  72.5 1.5 %bitcast_convert_fusion = f32[2048,256]{1,0:T(8,128)} fusion(bf16[8,2,128,256]{3,2,1,0:T(8,128)(2,1)S(1)} %get-tuple-element.17), kind=kLoop, calls=%fused_computation | loop fusion | flops 524288 | bytes 3145728 | tf_op jit(solution)/shard_map/convert_element_type | solution.py:377
  74.0 0.7 copy.18
  74.7 0.7 copy.19
  75.4 0.7 copy.20
  76.1 0.8 %copy.21 = f32[64,2048]{1,0:T(8,128)} copy(f32[64,2048]{1,0:T(8,128)S(1)} %get-tuple-element.28) | data formatting | bytes 1048576
Async XLA Ops:
  1.4 1.2 %copy-start = (bf16[2048,256]{1,0:T(8,128)(2,1)S(1)}, bf16[2048,256]{1,0:T(8,128)(2,1)}, u32[]{:S(2)}) copy-start(bf16[2048,256]{1,0:T(8,128)(2,1)} %w_head.1) | copy-start | bytes 3145732
  2.6 1.0 %copy-start.1 = (bf16[2,64,2048]{2,1,0:T(8,128)(2,1)S(1)}, bf16[2,64,2048]{2,1,0:T(8,128)(2,1)}, u32[]{:S(2)}) copy-start(bf16[2,64,2048]{2,1,0:T(8,128)(2,1)} %resid.1) | copy-start | bytes 1572868
  3.6 0.9 %copy-start.2 = (bf16[2,64,1024]{2,1,0:T(8,128)(2,1)S(1)}, bf16[2,64,1024]{2,1,0:T(8,128)(2,1)}, u32[]{:S(2)}) copy-start(bf16[2,64,1024]{2,1,0:T(8,128)(2,1)} %q.1) | copy-start | bytes 786436
  4.6 0.9 %copy-start.3 = (bf16[2,64,1024]{2,1,0:T(8,128)(2,1)S(1)}, bf16[2,64,1024]{2,1,0:T(8,128)(2,1)}, u32[]{:S(2)}) copy-start(bf16[2,64,1024]{2,1,0:T(8,128)(2,1)} %k.1) | copy-start | bytes 786436
  5.5 0.9 %copy-start.4 = (bf16[2,64,1024]{2,1,0:T(8,128)(2,1)S(1)}, bf16[2,64,1024]{2,1,0:T(8,128)(2,1)}, u32[]{:S(2)}) copy-start(bf16[2,64,1024]{2,1,0:T(8,128)(2,1)} %v.1) | copy-start | bytes 786436
  6.5 0.9 %copy-start.5 = (bf16[64,2048]{1,0:T(8,128)(2,1)S(1)}, bf16[64,2048]{1,0:T(8,128)(2,1)}, u32[]{:S(2)}) copy-start(bf16[64,2048]{1,0:T(8,128)(2,1)} %w_out.1) | copy-start | bytes 786436
  7.4 0.8 %copy-start.6 = (f32[64,256]{1,0:T(8,128)S(1)}, f32[64,256]{1,0:T(8,128)}, u32[]{:S(2)}) copy-start(f32[64,256]{1,0:T(8,128)} %target.1) | copy-start | bytes 196612

commit v2 on v1

--- a/solution.py
+++ b/solution.py
@@ -28,8 +28,10 @@
 
 def kernel(
     n,
-    q, k, v, resid, w_out, w_head, target, ids,
-    loss_o, dq_o, dk_o, dv_o, dwo_o, dwh_o,
+    q_in, k_in, v_in, resid_in, w_out_in, w_head_in, target_in, ids_in,
+    loss_out, dq_out, dk_out, dv_out, dwo_out, dwh_out,
+    loss_o, dq_o, dk_o, dv_o, dwo_o, dwh_o, out_sem,
+    q, k, v, resid, w_out, w_head, target, id_row, ids, in_sem,
     kw, vw, qw, idw, dpw, stw,
     m_all, pred0, bias, probs, att, dpred, da, stats, stats_t,
     ap_f, ap_b, ap_r1, ap_s2, ap_r2,
@@ -65,11 +67,35 @@
         copy.start()
         return copy
 
+    local = [
+        pltpu.make_async_copy(src, dst, in_sem.at[i])
+        for i, (src, dst) in enumerate((
+            (ids_in, id_row), (w_head_in, w_head), (w_out_in, w_out), (k_in, k), (resid_in, resid),
+            (q_in, q), (v_in, v), (target_in, target),
+        ))
+    ]
+    for copy in local:
+        copy.start()
+
+    written = []
+
+    def write(src, dst):
+        copy = pltpu.make_async_copy(src, dst, out_sem.at[len(written)])
+        copy.start()
+        written.append(copy)
+
     barrier = pltpu.get_barrier_semaphore()
     for to in [sib, outer] + [peer_chip(off) * 2 + par for off in range(1, nc)]:
         pl.semaphore_signal(
             barrier, inc=1, device_id={"seq": to}, device_id_type=pl.DeviceIdType.MESH
         )
+    local[0].wait()
+    square = (tok, tok)
+    diagonal = lax.broadcasted_iota(jnp.int32, square, 0) == lax.broadcasted_iota(jnp.int32, square, 1)
+    id_column = jnp.sum(
+        jnp.where(diagonal, id_row[...].astype(F32), 0.0), axis=1, keepdims=True
+    )
+    ids[...] = jnp.broadcast_to(id_column, ids.shape).astype(BF16)
     pl.semaphore_wait(barrier, nc + 1)
 
     pending = []
@@ -83,8 +109,10 @@
         return pair
 
     halo_id = halo(0, ids, idw)
-    halo_k = halo(1, k, kw)
-    halo_v = halo(2, v, vw)
+    halo_k = halo(1, k_in, kw)
+    halo_v = halo(2, v_in, vw)
+    local[1].wait()
+    local[2].wait()
 
     m_all[chip, par] = dot_nn(w_out[...], w_head[...]).astype(BF16)
     m_copies = [
@@ -93,7 +121,8 @@
         for off in range(1, nc)
     ]
     pending.extend(m_copies)
-    halo_q = halo(3, q, qw)
+    for copy in local[3:]:
+        copy.wait()
 
     pred0[...] = dot_nn(resid[...].reshape(members * tok, dm), w_head[...])
 
@@ -139,6 +168,7 @@
     pending.append(m_forward)
     for copy in halo_v:
         copy.wait_recv()
+    halo_q = halo(3, q_in, qw)
 
     def attend_step(step, _):
         for u in range(unroll):
@@ -220,6 +250,7 @@
 
     stats[...] = lax.fori_loop(0, heads // unroll, query_grad_step, lse)
     halo_s = halo(5, stats, stw)
+    write(dq_o, dq_out)
 
     for copy in ap_copies:
         copy.wait_recv()
@@ -236,6 +267,7 @@
     pending.append(g_pair)
     ap_low = (ap_total - ap_high.astype(F32)).astype(BF16)
     dwo_o[...] = dot_nt(ap_high, w_head[...]) + dot_nt(ap_low, w_head[...])
+    write(dwo_o, dwo_out)
     g_pair.wait_recv()
     g_copies = []
     for off in range(1, nc):
@@ -276,6 +308,8 @@
         return 0
 
     lax.fori_loop(0, heads // unroll, key_grad_step, 0)
+    write(dk_o, dk_out)
+    write(dv_o, dv_out)
 
     for copy in g_copies:
         copy.wait_recv()
@@ -283,26 +317,74 @@
     for off in range(1, nc):
         g_total = g_total + g_r2[off].astype(F32)
     dwh_o[chip, par] = g_total.astype(BF16)
-    ag_copies = [
-        remote(dwh_o.at[chip, par], dwh_o.at[chip, par], ag_ss.at[off], ag_rs.at[off],
-               peer_chip(off) * 2 + par)
-        for off in range(1, nc)
-    ]
-    pending.extend(ag_copies)
-    forwards = [remote(dwh_o.at[chip, par], dwh_o.at[chip, par], fw_ss.at[0], fw_rs.at[0], sib)]
+    outer_count = nc // 2
+    row, col = chip // 2, chip % 2
+    across = (row * 2 + 1 - col) * 2 + par
+    forwards, along, over = [], [], []
+
+    def send_on(c, off, to_across):
+        block = dwh_o.at[c, par]
+        if to_across:
+            over.append(
+                remote(block, block, ag_ss.at[outer_count + off], ag_rs.at[outer_count + off], across)
+            )
+        place = off if to_across else outer_count + off
+        forwards.append(remote(block, block, fw_ss.at[place], fw_rs.at[place], sib))
+
+    own = dwh_o.at[chip, par]
+    for off in range(1, outer_count):
+        to = (lax.rem(row + off, outer_count) * 2 + col) * 2 + par
+        along.append(remote(own, own, ag_ss.at[off], ag_rs.at[off], to))
+    send_on(chip, 0, True)
     for copy in loss_copies:
         copy.wait_recv()
-    loss_o[...] = jnp.sum(loss_all[...], axis=0)
-    for off in range(1, nc):
-        ag_copies[off - 1].wait_recv()
-        c = source_chip(off)
-        forwards.append(
-            remote(dwh_o.at[c, par], dwh_o.at[c, par], fw_ss.at[off], fw_rs.at[off], sib)
-        )
+    loss_o[...] = jnp.sum(loss_all[...], axis=0) / (n * tok * dpred.shape[1])
+    write(loss_o, loss_out)
+    for off in range(1, outer_count):
+        along[off - 1].wait_recv()
+        send_on(lax.rem(row + outer_count - off, outer_count) * 2 + col, off, True)
+    for off in range(outer_count):
+        over[off].wait_recv()
+        send_on(lax.rem(row + outer_count - off, outer_count) * 2 + 1 - col, off, False)
+    pending.extend(along + over)
     for copy in forwards:
         copy.wait_recv()
+    write(dwh_o, dwh_out)
     for copy in pending + forwards:
         copy.wait_send()
+    for copy in written:
+        copy.wait()
+
+
+def finish(loss, dq, dk, dv, dwo, dwh, loss_o, dq_o, dk_o, dv_o, dwo_o, dwh_o,
+           loss_v, dq_v, dk_v, dv_v, dwo_v, half, wide, sem):
+    parts = wide.shape[0]
+    plain = ((dwo, dwo_v, dwo_o), (dq, dq_v, dq_o), (dk, dk_v, dk_o), (dv, dv_v, dv_o))
+    load = [pltpu.make_async_copy(dwh.at[i], half.at[i], sem.at[i]) for i in range(parts)]
+    load += [
+        pltpu.make_async_copy(src, mid, sem.at[parts + i]) for i, (src, mid, _) in enumerate(plain)
+    ]
+    load.append(pltpu.make_async_copy(loss, loss_v, sem.at[parts + 4]))
+    for copy in load:
+        copy.start()
+    stores = []
+
+    def store(src, dst):
+        copy = pltpu.make_async_copy(src, dst, sem.at[parts + 5 + len(stores)])
+        copy.start()
+        stores.append(copy)
+
+    for i in range(parts):
+        load[i].wait()
+        wide[i] = half[i].astype(F32)
+        store(wide.at[i], dwh_o.at[i])
+    for i, (_, mid, dst) in enumerate(plain):
+        load[parts + i].wait()
+        store(mid, dst)
+    load[parts + 4].wait()
+    loss_o[0] = loss_v[0, 0]
+    for copy in stores:
+        copy.wait()
 
 
 def per_device(queries, keys, values, resid, w_out, w_head, target, block_ids):
@@ -312,11 +394,11 @@
     nc = n // 2
     dm, width = w_head.shape
     ar, gr = hd // n, dm // n
-    ids = jnp.broadcast_to(block_ids.astype(BF16)[:, None], (tok, DH))
-    vm = pl.BlockSpec(memory_space=pltpu.VMEM)
+    ids = block_ids.reshape(1, tok)
+    hbm = pl.BlockSpec(memory_space=pltpu.HBM)
     dma = pltpu.SemaphoreType.DMA
     like = jax.ShapeDtypeStruct(queries.shape, BF16)
-    loss, d_queries, d_keys, d_values, d_w_out, d_w_head = pl.pallas_call(
+    results = pl.pallas_call(
         functools.partial(kernel, n),
         out_shape=(
             jax.ShapeDtypeStruct((8, DH), F32),
@@ -324,9 +406,26 @@
             jax.ShapeDtypeStruct((ar, dm), F32),
             jax.ShapeDtypeStruct((nc, 2, gr, width), BF16),
         ),
-        in_specs=[vm] * 8,
-        out_specs=(vm,) * 6,
+        in_specs=[hbm] * 8,
+        out_specs=(hbm,) * 6,
         scratch_shapes=[
+            pltpu.VMEM((8, DH), F32),
+            pltpu.VMEM(queries.shape, BF16),
+            pltpu.VMEM(queries.shape, BF16),
+            pltpu.VMEM(queries.shape, BF16),
+            pltpu.VMEM((ar, dm), F32),
+            pltpu.VMEM((nc, 2, gr, width), BF16),
+            dma((6,)),
+            pltpu.VMEM(queries.shape, BF16),
+            pltpu.VMEM(queries.shape, BF16),
+            pltpu.VMEM(queries.shape, BF16),
+            pltpu.VMEM(resid.shape, BF16),
+            pltpu.VMEM(w_out.shape, BF16),
+            pltpu.VMEM(w_head.shape, BF16),
+            pltpu.VMEM(target.shape, F32),
+            pltpu.VMEM((1, tok), jnp.int32),
+            pltpu.VMEM((tok, DH), BF16),
+            dma((8,)),
             pltpu.VMEM((2,) + keys.shape, BF16),
             pltpu.VMEM((2,) + keys.shape, BF16),
             pltpu.VMEM((2,) + keys.shape, BF16),
@@ -365,17 +464,38 @@
             dma((nc,)), dma((nc,)),
         ],
         compiler_params=pltpu.CompilerParams(
-            collective_id=0, has_side_effects=True, vmem_limit_bytes=48 * 1024 * 1024
+            collective_id=0, has_side_effects=True, vmem_limit_bytes=60 * 1024 * 1024
         ),
         cost_estimate=pl.CostEstimate(
             flops=2_000_000_000, bytes_accessed=6_000_000, transcendentals=1_000_000
         ),
     )(queries, keys, values, resid, w_out, w_head, target, ids)
-    loss = (loss[0, 0] / (n * tok * width)).reshape(1)
-    return (
-        loss, d_queries, d_keys, d_values, d_w_out,
-        d_w_head.reshape(dm, width).astype(F32),
-    )
+    parts = 4
+    rows = dm // parts
+    loss, d_queries, d_keys, d_values, d_w_out, d_w_head = pl.pallas_call(
+        finish,
+        out_shape=(
+            jax.ShapeDtypeStruct((1,), F32),
+            like, like, like,
+            jax.ShapeDtypeStruct((ar, dm), F32),
+            jax.ShapeDtypeStruct((parts, rows, width), F32),
+        ),
+        in_specs=[hbm] * 6,
+        out_specs=(pl.BlockSpec(memory_space=pltpu.SMEM),) + (hbm,) * 5,
+        scratch_shapes=[
+            pltpu.VMEM((8, DH), F32),
+            pltpu.VMEM(queries.shape, BF16),
+            pltpu.VMEM(queries.shape, BF16),
+            pltpu.VMEM(queries.shape, BF16),
+            pltpu.VMEM((ar, dm), F32),
+            pltpu.VMEM((parts, rows, width), BF16),
+            pltpu.VMEM((parts, rows, width), F32),
+            dma((9 + 2 * parts,)),
+        ],
+        compiler_params=pltpu.CompilerParams(vmem_limit_bytes=60 * 1024 * 1024),
+        cost_estimate=pl.CostEstimate(flops=1_000_000, bytes_accessed=6_000_000, transcendentals=0),
+    )(*results[:5], results[5].reshape(parts, rows, width))
+    return (loss, d_queries, d_keys, d_values, d_w_out, d_w_head.reshape(dm, width))
 
 
 def solution(mesh):

time: 78.4 us -> 68.6 us (0.87)
  the two profiles are of different devices: /device:TPU:27 before, /device:TPU:0 now
where the time goes in v2:
time: 68.6 us; the launch traced here: 67.7 us
  Pallas kernels  67.1 us (98%)
    pallas_call x1, Pallas kernels, per_device(): pl.pallas_call(functools.partial(kernel, n), out_shape=(jax.ShapeDtypeStr...  63.7 us
    pallas_call x1, Pallas kernels, per_device(): pl.pallas_call(finish, out_shape=(jax.ShapeDtypeStruct((1,), F32), like,...  3.39 us

profile of v2, /device:TPU:0, one launch (start us, length us, event | category | flops | bytes accessed | tf_op | source)
XLA Modules:
  0.0 67.7 jit_solution(15275390750411548623)
XLA Ops:
  0.6 63.7 %shard_map.127 = (f32[8,128]{1,0:T(8,128)}, bf16[2,64,1024]{2,1,0:T(8,128)(2,1)}, bf16[2,64,1024]{2,1,0:T(8,128)(2,1)}, bf16[2,64,1024]{2,1,0:T(8,128)(2,1)}, f3...) custom-call(bf16[2,64,1024]{2,1,0:T(8,128)(2,1)} %q_in.1, bf16[2,64,1024]{2,1,0:T(8,128)(2,1)} %k_in.1, ...), custom_call_target="tpu_custom_call" | custom-call | flops 2000000000 | bytes 6000000 | tf_op jit(solution)/shard_map/pallas_call | solution.py:401
  64.3 3.4 %shard_map.128 = (f32[1]{0:T(128)}, bf16[2,64,1024]{2,1,0:T(8,128)(2,1)}, bf16[2,64,1024]{2,1,0:T(8,128)(2,1)}, bf16[2,64,1024]{2,1,0:T(8,128)(2,1)}, f32[64,2048]{1,0:T(8,128)}, /*index=5*/f32[4,512,256]{2,1,0:T(8,128)}) custom-call(f32[8,128]{1,0:T(8,128)} %get-tuple-element.18.loss, bf16[2,64,1024]{2,1,0:T(8,128)(2,1)} %get-tuple-element.19.dq, ...), custom_call_target="tpu_custom_call" | custom-call | flops 1000000 | bytes 6000000 | tf_op jit(solution)/shard_map/pallas_call | solution.py:475

commit v3 on v2

--- a/solution.py
+++ b/solution.py
@@ -322,30 +322,47 @@
     across = (row * 2 + 1 - col) * 2 + par
     forwards, along, over = [], [], []
 
-    def send_on(c, off, to_across):
-        block = dwh_o.at[c, par]
+    split = 2
+    piece = gr // split
+
+    def block_of(c, part):
+        return dwh_o.at[c, par, pl.ds(part * piece, piece)]
+
+    def send_on(c, off, part, to_across):
+        block = block_of(c, part)
         if to_across:
-            over.append(
-                remote(block, block, ag_ss.at[outer_count + off], ag_rs.at[outer_count + off], across)
-            )
-        place = off if to_across else outer_count + off
-        forwards.append(remote(block, block, fw_ss.at[place], fw_rs.at[place], sib))
-
-    own = dwh_o.at[chip, par]
-    for off in range(1, outer_count):
-        to = (lax.rem(row + off, outer_count) * 2 + col) * 2 + par
-        along.append(remote(own, own, ag_ss.at[off], ag_rs.at[off], to))
-    send_on(chip, 0, True)
+            at = (outer_count + off) * split + part
+            over.append(remote(block, block, ag_ss.at[at], ag_rs.at[at], across))
+        at = (off if to_across else outer_count + off) * split + part
+        forwards.append(remote(block, block, fw_ss.at[at], fw_rs.at[at], sib))
+
+    for part in range(split):
+        own = block_of(chip, part)
+        for off in range(1, outer_count):
+            to = (lax.rem(row + off, outer_count) * 2 + col) * 2 + par
+            at = off * split + part
+            along.append(remote(own, own, ag_ss.at[at], ag_rs.at[at], to))
+    for part in range(split):
+        send_on(chip, 0, part, True)
     for copy in loss_copies:
         copy.wait_recv()
     loss_o[...] = jnp.sum(loss_all[...], axis=0) / (n * tok * dpred.shape[1])
     write(loss_o, loss_out)
-    for off in range(1, outer_count):
-        along[off - 1].wait_recv()
-        send_on(lax.rem(row + outer_count - off, outer_count) * 2 + col, off, True)
-    for off in range(outer_count):
-        over[off].wait_recv()
-        send_on(lax.rem(row + outer_count - off, outer_count) * 2 + 1 - col, off, False)
+    arrived = iter(along)
+    for part in range(split):
+        for off in range(1, outer_count):
+            next(arrived).wait_recv()
+            send_on(
+                lax.rem(row + outer_count - off, outer_count) * 2 + col, off, part, True
+            )
+    arrived = iter(list(over))
+    for off, part in [(0, part) for part in range(split)] + [
+        (off, part) for part in range(split) for off in range(1, outer_count)
+    ]:
+        next(arrived).wait_recv()
+        send_on(
+            lax.rem(row + outer_count - off, outer_count) * 2 + 1 - col, off, part, False
+        )
     pending.extend(along + over)
     for copy in forwards:
         copy.wait_recv()
@@ -459,8 +476,8 @@
             dma((4,)), dma((4,)),
             dma((nc,)), dma((nc,)),
             dma((nc,)), dma((nc,)),
-            dma((nc,)), dma((nc,)),
-            dma((nc,)), dma((nc,)),
+            dma((2 * nc,)), dma((2 * nc,)),
+            dma((2 * nc,)), dma((2 * nc,)),
             dma((nc,)), dma((nc,)),
         ],
         compiler_params=pltpu.CompilerParams(

time: 68.6 us -> 69.6 us (1.015); the launches traced: 67.7 us -> 69.4 us
  Pallas kernels: 67.1 us -> 68.8 us
    pallas_call x1, Pallas kernels: 63.7 us -> 65.4 us  [per_device(): pl.pallas_call(functools.partial(kernel, n), out_shape=(jax.ShapeDtypeStr...]
where the time goes in v3:
time: 69.6 us; the launch traced here: 69.4 us
  Pallas kernels  68.8 us (99%)
    pallas_call x1, Pallas kernels, per_device(): pl.pallas_call(functools.partial(kernel, n), out_shape=(jax.ShapeDtypeStr...  65.4 us
    pallas_call x1, Pallas kernels, per_device(): pl.pallas_call(finish, out_shape=(jax.ShapeDtypeStruct((1,), F32), like,...  3.39 us

profile of v3, /device:TPU:0, one launch (start us, length us, event | category | flops | bytes accessed | tf_op | source)
XLA Modules:
  0.0 69.4 jit_solution(12382707173381981861)
XLA Ops:
  0.6 65.4 %shard_map.127 = (f32[8,128]{1,0:T(8,128)}, bf16[2,64,1024]{2,1,0:T(8,128)(2,1)}, bf16[2,64,1024]{2,1,0:T(8,128)(2,1)}, bf16[2,64,1024]{2,1,0:T(8,128)(2,1)}, f3...) custom-call(bf16[2,64,1024]{2,1,0:T(8,128)(2,1)} %q_in.1, bf16[2,64,1024]{2,1,0:T(8,128)(2,1)} %k_in.1, ...), custom_call_target="tpu_custom_call" | custom-call | flops 2000000000 | bytes 6000000 | tf_op jit(solution)/shard_map/pallas_call | solution.py:418
  66.0 3.4 %shard_map.128 = (f32[1]{0:T(128)}, bf16[2,64,1024]{2,1,0:T(8,128)(2,1)}, bf16[2,64,1024]{2,1,0:T(8,128)(2,1)}, bf16[2,64,1024]{2,1,0:T(8,128)(2,1)}, f32[64,2048]{1,0:T(8,128)}, /*index=5*/f32[4,512,256]{2,1,0:T(8,128)}) custom-call(f32[8,128]{1,0:T(8,128)} %get-tuple-element.18.loss, bf16[2,64,1024]{2,1,0:T(8,128)(2,1)} %get-tuple-element.19.dq, ...), custom_call_target="tpu_custom_call" | custom-call | flops 1000000 | bytes 6000000 | tf_op jit(solution)/shard_map/pallas_call | solution.py:492
